TPU v7x, 32 devices: a whole 2x2x4 slice. The times are simulated.
32 devices in a mesh: tower: 2 (over y), narrow: 4 (over z), wide: 4 (over x, core).
Axes of the slice: x: 2, y: 2, z: 4, core: 2. Of those that a mesh axis runs over, the one named last changes fastest.
Arguments:
- features: bfloat16 [4, 8, 256, 2048], P('narrow', ('tower', 'wide')), may hold values from -6 to 6
- w_in: bfloat16 [2048, 4096], P(None, 'narrow'), may hold values from -0.125 to 0.125
- b_in: float32 [4096], P('narrow'), may hold values from -0.5 to 0.5
- w_out: bfloat16 [4096, 256], P('narrow'), may hold values from -0.09375 to 0.09375
- user_emb: bfloat16 [8192, 256], P('narrow'), as said below
- item_ids: int32 [4, 8, 256], P('narrow', ('tower', 'wide')), may hold values from 0 to 8191
Outputs:
- row_loss: float32 [8192], P('narrow')
- item_grad: float32 [4, 8, 256, 256], P('narrow', ('tower', 'wide'))
Inputs may be any that keep to these rules, and one draw needn't show every extreme that they name: `user_emb`: user embeddings.
All inputs are finite; a program needn't handle non-finite values.
Results may differ from a plain program's by a relative error of at most 0.024.
Values may be sent and summed in bfloat16 or wider, within the bound.
A program may use at most 64 MiB of HBM per device.

v0:
```python
import jax
import jax.numpy as jnp
from jax import lax
from jax.sharding import PartitionSpec as P

INV_TEMP = 4.0
EPS = 1e-06
NEG = -1e30


def unit_rows(embed):
    return embed * lax.rsqrt(jnp.sum(embed * embed, axis=1, keepdims=True) + EPS)


def block_scores(user, rid, rglob, vectors, col_ids, col_glob):
    scores = (
        lax.dot_general(user, vectors, (((1,), (1,)), ((), ())), preferred_element_type=jnp.float32)
        * INV_TEMP
    )
    diag = rglob[:, None] == col_glob[None, :]
    keep = (rid[:, None] != col_ids[None, :]) | diag
    return (scores, diag, keep)


def block_scores_cols(vectors, col_ids, col_glob, user, rid, rglob):
    scores = (
        lax.dot_general(vectors, user, (((1,), (1,)), ((), ())), preferred_element_type=jnp.float32)
        * INV_TEMP
    )
    diag = col_glob[:, None] == rglob[None, :]
    keep = (col_ids[:, None] != rid[None, :]) | diag
    return (scores, diag, keep)


def local(features, w_in, b_in, w_out, user_emb, item_ids):
    share = features.shape[2]
    width = features.shape[3]
    embed_width = w_out.shape[1]
    users_dev = user_emb.shape[0]
    groups = lax.axis_size("narrow")
    panel = groups * share
    gathered, gathered_ids = (
        lax.all_gather(features, "narrow", axis=0, tiled=True),
        lax.all_gather(item_ids, "narrow", axis=0, tiled=True),
    )
    rows_in = gathered.reshape(panel, width)
    col_ids = gathered_ids.reshape(panel)
    hidden = jax.nn.relu(jnp.dot(rows_in, w_in, preferred_element_type=jnp.float32) + b_in).astype(
        jnp.bfloat16
    )
    partial_embed = jnp.dot(hidden, w_out, preferred_element_type=jnp.float32)
    item_vec = unit_rows(lax.psum(partial_embed, "narrow")).astype(jnp.bfloat16)
    row_ids = lax.all_gather(item_ids, ("tower", "wide"), axis=1, tiled=True).reshape(users_dev)
    narrow_index = lax.axis_index("narrow")
    panel_index = lax.axis_index(("tower", "wide"))
    row_glob = narrow_index * users_dev + jnp.arange(users_dev, dtype=jnp.int32)
    column = jnp.arange(panel, dtype=jnp.int32)
    col_glob = column // share * users_dev + panel_index * share + column % share
    block = min(512, users_dev)
    count = users_dev // block
    users = user_emb.reshape(count, block, embed_width)
    rid_blocks = row_ids.reshape(count, block)
    rglob_blocks = row_glob.reshape(count, block)

    def local_stats(blk):
        user, rid, rglob = blk
        scores, diag, keep = block_scores(user, rid, rglob, item_vec, col_ids, col_glob)
        masked = jnp.where(keep, scores, NEG)
        top = jnp.max(masked, axis=1)
        mass = jnp.sum(jnp.where(keep, jnp.exp(scores - top[:, None]), 0.0), axis=1)
        pos = jnp.sum(jnp.where(diag, scores, 0.0), axis=1)
        return (top, mass, pos, masked.T)

    def local_stats_only(blk):
        top, mass, pos, masked = local_stats(blk)
        return (top, mass, pos)

    top, mass, pos = lax.map(local_stats_only, (users, rid_blocks, rglob_blocks))
    top = top.reshape(users_dev)
    mass = mass.reshape(users_dev)
    pos = pos.reshape(users_dev)
    global_top = lax.pmax(top, ("tower", "wide"))
    total, global_pos = lax.psum((mass * jnp.exp(top - global_top), pos), ("tower", "wide"))
    lse = global_top + jnp.log(total)
    row_loss = lse - global_pos
    lse_blocks = lse.reshape(count, block)

    def add_block(acc, blk):
        user, rid, rglob, lse_blk = blk
        scores, diag, keep = block_scores_cols(item_vec, col_ids, col_glob, user, rid, rglob)
        coef = (
            jnp.where(keep, jnp.exp(scores - lse_blk[None, :]), 0.0) - diag.astype(jnp.float32)
        ).astype(jnp.bfloat16)
        term = jnp.dot(coef, user, preferred_element_type=jnp.float32)
        return (acc + term, None)

    acc, unused = lax.scan(
        add_block,
        jnp.zeros((share * lax.axis_size("narrow"), embed_width), jnp.float32),
        (users, rid_blocks, rglob_blocks, lse_blocks),
    )
    own_grad = lax.psum_scatter(INV_TEMP * acc, "narrow", scatter_dimension=0, tiled=True)
    return (row_loss, own_grad.reshape(1, 1, share, embed_width))


def solution(mesh):
    return jax.shard_map(
        local,
        mesh=mesh,
        in_specs=(
            P("narrow", ("tower", "wide"), None, None),
            P(None, "narrow"),
            P("narrow"),
            P("narrow", None),
            P("narrow", None),
            P("narrow", ("tower", "wide"), None),
        ),
        out_specs=(P("narrow"), P("narrow", ("tower", "wide"), None, None)),
        check_vma=False,
    )
```

profile of v0, /device:TPU:0, one launch (start us, length us, event | category | flops | bytes accessed | tf_op | source)
XLA Modules:
  0.0 238.5 jit_solution(5663523277225741020)
XLA Ops:
  7.2 0.0 copy-start
  7.2 0.0 all-gather.2.cloned.1.call-start
  7.2 0.7 all-gather.2.cloned.1.call-update
  7.9 0.0 all-reduce.3.cloned.1.call-start
  8.0 85.1 %all-gather.2.cloned.1.call-done = bf16[4,1,256,2048]{3,2,1,0:T(8,128)(2,1)} async-done(((bf16[1,1,256,2048]{3,2,1,0:T(8,128)(2,1)}), bf16[4,1,256,2048]{3,2,1,0:T(8,128)(2,1)}) %all-gather.2.cloned.1.call-update) | async-done | bytes 4194320 | tf_op jit(solution)/shard_map/all_gather | solution.py:43
  93.1 0.0 copy-done
  93.1 0.0 copy-start.1
  93.1 9.6 %fusion.48 = f32[1024,256]{1,0:T(8,128)} fusion(bf16[1024,256]{1,0:T(8,128)(2,1)S(1)} %copy-done, f32[1024]{0:T(1024)} %param.12, bf16[1024,2048]{1,0:T(8,128)(2,1)} %bitcast.95, bf16[2048,1024]{1,0:T(8,128)(2,1)} %param.11), kind=kOutput, calls=%fused_computation.64 | convolution fusion | flops 4834983936 | bytes 9965568 | tf_op jit(solution)/shard_map/dot_general | solution.py:51
  102.7 0.0 copy-start.2
  102.7 0.0 all-reduce.3.cloned.1.call-update
  102.7 0.0 reduce-scatter.2.cloned.1.call-start
  102.8 0.0 copy-done.1
  102.8 9.0 %all_gather.9 = s32[1,8,256]{2,0,1:T(1,128)S(1)} all-gather(s32[1,1,256]{2,0,1:T(1,128)S(1)} %bitcast.94), channel_id=1, replica_groups=mesh['tower'=2,'narrow'=4,'wide'=4] {'tower','wide'}, dimensions={1}, use_global_device_ids=true | all-gather | bytes 9216 | tf_op jit(solution)/shard_map/all_gather | solution.py:53
  111.9 8.8 %all_gather.10 = s32[4,1,256]{2,1,0:T(1,128)S(1)} all-gather(s32[1,1,256]{2,1,0:T(1,128)S(1)} %copy-done.1), channel_id=1, replica_groups=mesh['tower'=2,'narrow'=4,'wide'=4] {'narrow'}, dimensions={0}, use_global_device_ids=true | all-gather | bytes 5120 | tf_op jit(solution)/shard_map/all_gather | solution.py:44
  120.7 32.6 %all-reduce.3.cloned.1.call-done = f32[1024,256]{1,0:T(8,128)} async-done(((f32[1024,256]{1,0:T(8,128)}), f32[1024,256]{1,0:T(8,128)}) %all-reduce.3.cloned.1.call-update) | async-done | bytes 1048592 | tf_op jit(solution)/shard_map/psum | solution.py:52
  153.3 1.4 multiply_reduce_fusion
  154.8 1.4 multiply_convert_fusion
  156.2 0.0 copy-done.2
  156.2 7.8 %while.26 = (s32[]{:T(128)}, f32[4,512]{1,0:T(4,128)S(1)}, f32[4,512]{1,0:T(4,128)S(1)}, f32[4,512]{1,0:T(4,128)S(1)}, s32[4,512]{1,0:T(4,128)S(1)}, /*index=5*/...) while((s32[]{:T(128)}, f32[4,512]{1,0:T(4,128)S(1)}, ...), condition=%wide.region_6.7_spmd.clone, body=%wide.region_2.6_spmd.clone.sunk | while | flops 276313600 | bytes 5038221 | solution.py:78
  156.2 0.7 select_reduce_fusion.3
  156.9 1.1 fusion.70
  158.0 0.1 dynamic_update_slice.17
  158.1 0.1 dynamic_update_slice.16
  158.2 0.7 select_reduce_fusion.3
  158.9 1.1 fusion.70
  160.0 0.1 dynamic_update_slice.17
  160.0 0.1 dynamic_update_slice.16
  160.1 0.7 select_reduce_fusion.3
  160.8 1.1 fusion.70
  162.0 0.1 dynamic_update_slice.17
  162.0 0.1 dynamic_update_slice.16
  162.1 0.7 select_reduce_fusion.3
  162.8 1.1 fusion.70
  163.9 0.1 dynamic_update_slice.17
  164.0 0.1 dynamic_update_slice.16
  164.0 14.1 %pmax.7 = f32[2048]{0:T(1024)S(1)} all-reduce(f32[2048]{0:T(1024)S(1)} %bitcast.84), channel_id=1, replica_groups=mesh['tower'=2,'narrow'=4,'wide'=4] {'tower','wide'}, use_global_device_ids=true, to_apply=%region_7.8 | all-reduce | flops 2048 | bytes 16384 | tf_op jit(solution)/shard_map/pmax | solution.py:82
  178.2 22.3 %all-reduce = (f32[2048]{0:T(1024)S(1)}, f32[2048]{0:T(1024)S(1)}) all-reduce(f32[2048]{0:T(1024)S(1)} %exponential_multiply_fusion, f32[2048]{0:T(1024)S(1)} %bitcast.89), channel_id=1, replica_groups=mesh['tower'=2,'narrow'=4,'wide'=4] {'tower','wide'}, use_global_device_ids=true, to_apply=%region_8.9 | all-reduce | flops 4096 | bytes 32768 | tf_op jit(solution)/shard_map/psum | solution.py:83
  200.5 0.6 fusion.54
  201.1 4.9 %while.27 = (s32[]{:T(128)}, f32[1024,256]{1,0:T(8,128)S(1)}, s32[4,1,256]{2,1,0:T(1,128)S(1)}, s32[4,512]{1,0:T(4,128)S(1)}, s32[4,512]{1,0:T(4,128)S(1)}, /*in...) while((s32[]{:T(128)}, f32[1024,256]{1,0:T(8,128)S(1)}, ...), condition=%wide.region_11.12_spmd.clone, body=%wide.region_10.11_spmd.clone.sunk | while | flops 542129152 | bytes 3177603 | solution.py:97
  201.2 1.2 fusion.75
  202.4 1.2 fusion.75
  203.7 1.2 fusion.75
  204.9 1.2 fusion.75
  206.1 1.1 broadcast_multiply_fusion
  207.1 0.0 reduce-scatter.2.cloned.1.call-update
  207.2 24.8 %reduce-scatter.2.cloned.1.call-done = f32[256,256]{1,0:T(8,128)} async-done(((f32[1024,256]{1,0:T(8,128)}), f32[256,256]{1,0:T(8,128)}) %reduce-scatter.2.cloned.1.call-update) | async-done | bytes 262160 | tf_op jit(solution)/shard_map/reduce_scatter | solution.py:102
  (37 shorter events, 0.5 us)
Async XLA Ops:
  7.2 85.9 %copy-start = (bf16[1024,256]{1,0:T(8,128)(2,1)S(1)}, bf16[1024,256]{1,0:T(8,128)(2,1)}, u32[]{:S(2)}) copy-start(bf16[1024,256]{1,0:T(8,128)(2,1)} %param.13) | copy-start | bytes 1572868
  7.2 85.9 %all-gather.2.cloned.1.call-start = ((), (), s32[]{:S(2)}) async-start(), calls=%async_computation.1 | async-start | bytes 5242880 | tf_op jit(solution)/shard_map/all_gather | solution.py:43
  7.9 145.4 %all-reduce.3.cloned.1.call-start = ((), (), s32[]{:S(2)}) async-start(), calls=%async_computation.2 | async-start | bytes 2097152 | tf_op jit(solution)/shard_map/psum | solution.py:52
  93.1 9.8 %copy-start.1 = (s32[1,1,256]{2,1,0:T(1,128)S(1)}, s32[1,1,256]{2,1,0:T(1,128)}, u32[]{:S(2)}) copy-start(s32[1,1,256]{2,1,0:T(1,128)} %param.15) | copy-start | bytes 3076
  102.7 53.5 %copy-start.2 = (bf16[2048,256]{1,0:T(8,128)(2,1)S(1)}, bf16[2048,256]{1,0:T(8,128)(2,1)}, u32[]{:S(2)}) copy-start(bf16[2048,256]{1,0:T(8,128)(2,1)} %param.14) | copy-start | bytes 3145732
  102.7 129.3 %reduce-scatter.2.cloned.1.call-start = ((), (), s32[]{:S(2)}) async-start(), calls=%async_computation.3 | async-start | bytes 1310720 | tf_op jit(solution)/shard_map/reduce_scatter | solution.py:102
Sparse Core Ops, SparseCore 0:
  9.6 83.4 all-gather.1
  102.9 50.3 all-reduce.2
  207.3 24.6 reduce-scatter.1
where the time goes:
time: 239 us
  waiting for transfers between devices  143 us (60%)
  blocking collectives  54.2 us (23%)
  matrix products  17 us (7%)
  between operations  13.9 us (6%)
  other arithmetic  8.95 us (4%)
    all_gather x1, waiting for transfers between devices, local(): lax.all_gather(features, 'narrow', axis=0, tiled=True)  85.1 us
    psum x1, waiting for transfers between devices, local(): item_vec = unit_rows(lax.psum(partial_embed, 'narrow')).astype(jnp.bfloat16)  32.6 us
    reduce_scatter x1, waiting for transfers between devices, local(): lax.psum_scatter(INV_TEMP * acc, 'narrow', scatter_dimension=0, tiled=True)  24.8 us
    psum x1, blocking collectives, local(): lax.psum((mass * jnp.exp(top - global_top), pos), ('tower', 'wide'))  22.3 us
    pmax x1, blocking collectives, local(): global_top = lax.pmax(top, ('tower', 'wide'))  14.1 us
    dot_general x1, matrix products, local(): partial_embed = jnp.dot(hidden, w_out, preferred_element_type=jnp.float32)  9.62 us
    all_gather x1, blocking collectives, local(): lax.all_gather(item_ids, ('tower', 'wide'), axis=1, tiled=True)  9.02 us
    all_gather x1, blocking collectives, local(): lax.all_gather(item_ids, 'narrow', axis=0, tiled=True)  8.76 us
  transfers between devices with their start and end apart: 3, of which 3 were waited for; matrix products, arithmetic and copies ran while one was open for 0% of the time, Pallas kernels for 0%

commit v1 on v0

--- a/solution.py
+++ b/solution.py
@@ -49,7 +49,9 @@
         jnp.bfloat16
     )
     partial_embed = jnp.dot(hidden, w_out, preferred_element_type=jnp.float32)
-    item_vec = unit_rows(lax.psum(partial_embed, "narrow")).astype(jnp.bfloat16)
+    item_vec = unit_rows(jnp.sum(lax.all_gather(partial_embed, "narrow"), axis=0)).astype(
+        jnp.bfloat16
+    )
     row_ids = lax.all_gather(item_ids, ("tower", "wide"), axis=1, tiled=True).reshape(users_dev)
     narrow_index = lax.axis_index("narrow")
     panel_index = lax.axis_index(("tower", "wide"))

time: 239 us -> 275 us (1.15)
  waiting for transfers between devices: 143 us -> 172 us
  matrix products: 17 us -> 24.9 us
    all_gather x0 -> x1, waiting for transfers between devices: none -> 61.9 us  [local(): lax.all_gather(partial_embed, 'narrow')]
    psum x1 -> x0, waiting for transfers between devices: 32.6 us -> none  [local(): item_vec = unit_rows(lax.psum(partial_embed, 'narrow')).astype(jnp.bfloat16)]
    dot_general x4, matrix products: 4.65 us -> 8.79 us  [add_block(): term = jnp.dot(coef, user, preferred_element_type=jnp.float32)]
    dot_general x4, matrix products: 2.7 us -> 6.51 us  [block_scores(): lax.dot_general(user, vectors, (((1,), (1,)), ((), ())), preferred_elemen...]
where the time goes in v1:
time: 275 us
  waiting for transfers between devices  172 us (63%)
  blocking collectives  53.7 us (20%)
  matrix products  24.9 us (9%)
  between operations  13.9 us (5%)
  other arithmetic  9.14 us (3%)
    all_gather x1, waiting for transfers between devices, local(): lax.all_gather(features, 'narrow', axis=0, tiled=True)  85.1 us
    all_gather x1, waiting for transfers between devices, local(): lax.all_gather(partial_embed, 'narrow')  61.9 us
    reduce_scatter x1, waiting for transfers between devices, local(): lax.psum_scatter(INV_TEMP * acc, 'narrow', scatter_dimension=0, tiled=True)  24.1 us
    psum x1, blocking collectives, local(): lax.psum((mass * jnp.exp(top - global_top), pos), ('tower', 'wide'))  22.3 us
    pmax x1, blocking collectives, local(): global_top = lax.pmax(top, ('tower', 'wide'))  13.9 us
    dot_general x1, matrix products, local(): partial_embed = jnp.dot(hidden, w_out, preferred_element_type=jnp.float32)  9.62 us
    all_gather x1, blocking collectives, local(): lax.all_gather(item_ids, ('tower', 'wide'), axis=1, tiled=True)  8.89 us
    dot_general x4, matrix products, add_block(): term = jnp.dot(coef, user, preferred_element_type=jnp.float32)  8.79 us
  transfers between devices with their start and end apart: 3, of which 3 were waited for; matrix products, arithmetic and copies ran while one was open for 0% of the time, Pallas kernels for 0%

profile of v1, /device:TPU:0, one launch (start us, length us, event | category | flops | bytes accessed | tf_op | source)
XLA Modules:
  0.0 274.6 jit_solution(12173689838555381951)
XLA Ops:
  7.2 0.0 copy-start
  7.2 0.0 all-gather.4.cloned.1.call-start
  7.2 0.7 all-gather.4.cloned.1.call-update
  7.9 0.0 all-gather.6.cloned.1.call-start
  8.0 85.1 %all-gather.4.cloned.1.call-done = bf16[4,1,256,2048]{3,2,1,0:T(8,128)(2,1)} async-done(((bf16[1,1,256,2048]{3,2,1,0:T(8,128)(2,1)}), bf16[4,1,256,2048]{3,2,1,0:T(8,128)(2,1)}) %all-gather.4.cloned.1.call-update) | async-done | bytes 4194320 | tf_op jit(solution)/shard_map/all_gather | solution.py:43
  93.1 0.0 copy-done
  93.1 0.0 copy-start.1
  93.1 9.6 %fusion.48 = f32[1024,256]{1,0:T(8,128)} fusion(bf16[1024,256]{1,0:T(8,128)(2,1)S(1)} %copy-done, f32[1024]{0:T(1024)} %param.12, bf16[1024,2048]{1,0:T(8,128)(2,1)} %bitcast.97, bf16[2048,1024]{1,0:T(8,128)(2,1)} %param.11), kind=kOutput, calls=%fused_computation.64 | convolution fusion | flops 4834983936 | bytes 9965568 | tf_op jit(solution)/shard_map/dot_general | solution.py:51
  102.7 0.0 all-gather.6.cloned.1.call-update
  102.7 0.0 reduce-scatter.2.cloned.1.call-start
  102.8 0.0 copy-done.1
  102.8 8.9 %all_gather.15 = s32[1,8,256]{2,0,1:T(1,128)S(1)} all-gather(s32[1,1,256]{2,0,1:T(1,128)S(1)} %bitcast.96), channel_id=1, replica_groups=mesh['tower'=2,'narrow'=4,'wide'=4] {'tower','wide'}, dimensions={1}, use_global_device_ids=true | all-gather | bytes 9216 | tf_op jit(solution)/shard_map/all_gather | solution.py:55
  111.8 8.5 %all_gather.16 = s32[4,1,256]{2,1,0:T(1,128)S(1)} all-gather(s32[1,1,256]{2,1,0:T(1,128)S(1)} %copy-done.1), channel_id=1, replica_groups=mesh['tower'=2,'narrow'=4,'wide'=4] {'narrow'}, dimensions={0}, use_global_device_ids=true | all-gather | bytes 5120 | tf_op jit(solution)/shard_map/all_gather | solution.py:44
  120.3 61.9 %all-gather.6.cloned.1.call-done = f32[4096,256]{1,0:T(8,128)} async-done(((f32[1024,256]{1,0:T(8,128)}), f32[4096,256]{1,0:T(8,128)}) %all-gather.6.cloned.1.call-update) | async-done | bytes 4194320 | tf_op jit(solution)/shard_map/all_gather | solution.py:52
  182.2 2.6 reduce_sum.36
  184.8 0.2 multiply_reduce_fusion
  185.1 0.2 multiply_convert_fusion
  185.3 11.6 %while.26 = (s32[]{:T(128)}, f32[4,512]{1,0:T(4,128)S(1)}, f32[4,512]{1,0:T(4,128)S(1)}, f32[4,512]{1,0:T(4,128)S(1)}, s32[4,512]{1,0:T(4,128)S(1)}, /*index=5*/...) while((s32[]{:T(128)}, f32[4,512]{1,0:T(4,128)S(1)}, ...), condition=%wide.region_6.7_spmd.clone, body=%wide.region_2.6_spmd.clone.sunk | while | flops 276313600 | bytes 5038729 | solution.py:80
  185.3 1.6 select_reduce_fusion.3
  186.9 1.1 fusion.70
  188.1 0.1 dynamic_update_slice.17
  188.1 0.1 dynamic_update_slice.16
  188.2 1.6 select_reduce_fusion.3
  189.9 1.1 fusion.70
  191.0 0.1 dynamic_update_slice.17
  191.0 0.1 dynamic_update_slice.16
  191.1 1.6 select_reduce_fusion.3
  192.8 1.1 fusion.70
  193.9 0.1 dynamic_update_slice.17
  193.9 0.1 dynamic_update_slice.16
  194.0 1.6 select_reduce_fusion.3
  195.7 1.1 fusion.70
  196.8 0.1 dynamic_update_slice.17
  196.8 0.1 dynamic_update_slice.16
  196.9 13.9 %pmax.7 = f32[2048]{0:T(1024)S(1)} all-reduce(f32[2048]{0:T(1024)S(1)} %bitcast.86), channel_id=1, replica_groups=mesh['tower'=2,'narrow'=4,'wide'=4] {'tower','wide'}, use_global_device_ids=true, to_apply=%region_7.8 | all-reduce | flops 2048 | bytes 16384 | tf_op jit(solution)/shard_map/pmax | solution.py:84
  210.9 22.3 %all-reduce = (f32[2048]{0:T(1024)S(1)}, f32[2048]{0:T(1024)S(1)}) all-reduce(f32[2048]{0:T(1024)S(1)} %exponential_multiply_fusion, f32[2048]{0:T(1024)S(1)} %bitcast.91), channel_id=1, replica_groups=mesh['tower'=2,'narrow'=4,'wide'=4] {'tower','wide'}, use_global_device_ids=true, to_apply=%region_8.9 | all-reduce | flops 4096 | bytes 32768 | tf_op jit(solution)/shard_map/psum | solution.py:85
  233.2 0.6 fusion.54
  233.8 9.1 %while.27 = (s32[]{:T(128)}, f32[1024,256]{1,0:T(8,128)S(1)}, s32[4,1,256]{2,1,0:T(1,128)S(1)}, s32[4,512]{1,0:T(4,128)S(1)}, s32[4,512]{1,0:T(4,128)S(1)}, /*in...) while((s32[]{:T(128)}, f32[1024,256]{1,0:T(8,128)S(1)}, ...), condition=%wide.region_11.12_spmd.clone, body=%wide.region_10.11_spmd.clone.sunk | while | flops 542129152 | bytes 3177603 | solution.py:99
  233.9 2.2 fusion.75
  236.2 2.2 fusion.75
  238.5 2.2 fusion.75
  240.7 2.2 fusion.75
  242.9 1.1 broadcast_multiply_fusion
  244.0 0.0 reduce-scatter.2.cloned.1.call-update
  244.0 24.1 %reduce-scatter.2.cloned.1.call-done = f32[256,256]{1,0:T(8,128)} async-done(((f32[1024,256]{1,0:T(8,128)}), f32[256,256]{1,0:T(8,128)}) %reduce-scatter.2.cloned.1.call-update) | async-done | bytes 262160 | tf_op jit(solution)/shard_map/reduce_scatter | solution.py:104
  (37 shorter events, 0.5 us)
Async XLA Ops:
  7.2 85.9 %copy-start = (bf16[1024,256]{1,0:T(8,128)(2,1)S(1)}, bf16[1024,256]{1,0:T(8,128)(2,1)}, u32[]{:S(2)}) copy-start(bf16[1024,256]{1,0:T(8,128)(2,1)} %param.13) | copy-start | bytes 1572868
  7.2 85.9 %all-gather.4.cloned.1.call-start = ((), (), s32[]{:S(2)}) async-start(), calls=%async_computation.1 | async-start | bytes 5242880 | tf_op jit(solution)/shard_map/all_gather | solution.py:43
  7.9 174.3 %all-gather.6.cloned.1.call-start = ((), (), s32[]{:S(2)}) async-start(), calls=%async_computation.3 | async-start | bytes 5242880 | tf_op jit(solution)/shard_map/all_gather | solution.py:52
  93.1 9.7 %copy-start.1 = (s32[1,1,256]{2,1,0:T(1,128)S(1)}, s32[1,1,256]{2,1,0:T(1,128)}, u32[]{:S(2)}) copy-start(s32[1,1,256]{2,1,0:T(1,128)} %param.15) | copy-start | bytes 3076
  102.7 165.3 %reduce-scatter.2.cloned.1.call-start = ((), (), s32[]{:S(2)}) async-start(), calls=%async_computation.2 | async-start | bytes 1310720 | tf_op jit(solution)/shard_map/reduce_scatter | solution.py:104
Sparse Core Ops, SparseCore 0:
  9.6 83.4 all-gather.3
  102.9 79.3 all-gather.5
  244.1 23.9 reduce-scatter.1
